TPU v7x, 512 devices: a whole 4x8x8 slice. The times are simulated.
512 devices in a mesh: dp: 4 (over z_hi, core), ctx: 128 (over y, x, z_lo).
Axes of the slice: x: 4, y: 8, z: 8 (z_hi: 2, z_lo: 4; z = z_hi * 4 + z_lo), core: 2. Of those that a mesh axis runs over, the one named last changes fastest.
Arguments:
- queries: bfloat16 [4, 16384, 384], P('dp', 'ctx'), may hold values from -6 to 6
- keys: bfloat16 [4, 16384, 384], P('dp', 'ctx'), may hold values from -6 to 6
- values: bfloat16 [4, 16384, 384], P('dp', 'ctx'), may hold values from -6 to 6
- filter_taps: bfloat16 [16384, 384], P('ctx'), may hold values from -6 to 6
- cotangent: bfloat16 [4, 16384, 384], P('dp', 'ctx'), may hold values from -6 to 6
Outputs:
- gated: bfloat16 [4, 16384, 384], P('dp', 'ctx')
- grad_queries: bfloat16 [4, 16384, 384], P('dp', 'ctx')
- grad_keys: bfloat16 [4, 16384, 384], P('dp', 'ctx')
- grad_values: bfloat16 [4, 16384, 384], P('dp', 'ctx')
- filter_grad: float32 [16384, 384], P('ctx')
All inputs are finite; a program needn't handle non-finite values.
Results may differ from a plain program's by a relative error of at most 0.015.
Values may be sent and summed in bfloat16 or wider, within the bound.
A program may use at most 64 MiB of HBM per device.

v0:
```python
import functools

import jax
import jax.numpy as jnp
import numpy as np
from jax import lax
from jax.experimental import pallas as pl
from jax.experimental.pallas import tpu as pltpu
from jax.sharding import PartitionSpec as P

MESH = pl.DeviceIdType.MESH
BF16 = jnp.bfloat16
F32 = jnp.float32


def dot(left, right, contract=(1, 0)):
    dims = (((contract[0],), (contract[1],)), ((), ()))
    return lax.dot_general(left, right, dims, preferred_element_type=F32)


def constant_tables(group, rows):
    total = group * rows
    outer = np.arange(group)
    inner = np.arange(rows)
    angle_outer = 2 * np.pi * np.outer(outer + 0.25, outer) / group
    angle_twist = 2 * np.pi * np.outer(outer + 0.25, inner) / total
    angle_inner = 2 * np.pi * np.outer(inner, inner) / rows
    cos_outer, sin_outer = np.cos(angle_outer), np.sin(angle_outer)
    forward = np.zeros((2, 2, group, group, 2))
    inverse = np.zeros((group, 2, 2, 2, group))
    scale = 1.0 / (total * np.sqrt(total))
    for slot in range(2):
        forward[slot, 0, :, :, slot] = cos_outer
        forward[slot, 1, :, :, slot] = -sin_outer
        inverse[:, slot, slot, 0, :] = cos_outer.T * scale
        inverse[:, slot, slot, 1, :] = -sin_outer.T * scale
    cos_inner, sin_inner = np.cos(angle_inner), np.sin(angle_inner)
    inner_forward = np.block([[cos_inner, -sin_inner], [sin_inner, cos_inner]])
    inner_inverse = np.block([[cos_inner, sin_inner], [-sin_inner, cos_inner]])
    pick = np.zeros((group, 2, 2, group))
    for slot in range(2):
        pick[outer, slot, slot, outer] = 1.0
    return (
        jnp.asarray(forward.reshape(4 * group, 2 * group), BF16),
        jnp.asarray(inverse.reshape(2 * group, 4 * group), BF16),
        jnp.asarray(inner_forward, BF16),
        jnp.asarray(inner_inverse, BF16),
        jnp.asarray(pick.reshape(2 * group, 2 * group), BF16),
        jnp.asarray(np.cos(angle_twist), F32),
        jnp.asarray(np.sin(angle_twist), F32),
    )


def kernel(
    group,
    parts,
    queries,
    keys,
    values,
    taps,
    cotangent,
    forward_hbm,
    inverse_hbm,
    inner_forward_hbm,
    inner_inverse_hbm,
    pick_hbm,
    twist_cos_hbm,
    twist_sin_hbm,
    gated,
    grad_queries,
    grad_keys,
    grad_values,
    filter_grad,
    q_buf,
    k_buf,
    v_buf,
    t_buf,
    c_buf,
    forward,
    inverse,
    inner_forward,
    inner_inverse,
    pick,
    twist_cos,
    twist_sin,
    send_pair,
    recv_pair,
    send_taps,
    recv_taps,
    send_back,
    recv_back,
    send_filter,
    sum_filter,
    recv_filter,
    recv_parts,
    turned,
    spectrum,
    product,
    untwisted,
    in_sem,
    table_sem,
    copy_sem,
):
    me = lax.axis_index("ctx")
    part = lax.axis_index("dp")
    lanes = queries.shape[1] // group
    rows = queries.shape[0]

    loads = [
        pltpu.make_async_copy(source, target, in_sem.at[index])
        for index, (source, target) in enumerate(
            [(keys, k_buf), (values, v_buf), (queries, q_buf), (cotangent, c_buf), (taps, t_buf), (pick_hbm, pick)]
        )
    ]
    tables = [
        pltpu.make_async_copy(source, target, table_sem.at[index])
        for index, (source, target) in enumerate(
            [
                (forward_hbm, forward),
                (twist_cos_hbm, twist_cos),
                (twist_sin_hbm, twist_sin),
                (inner_forward_hbm, inner_forward),
                (inner_inverse_hbm, inner_inverse),
                (inverse_hbm, inverse),
            ]
        )
    ]
    for load in loads + tables:
        load.start()

    barrier = pltpu.get_barrier_semaphore()

    @pl.loop(1, group)
    def _(step):
        pl.semaphore_signal(
            barrier, inc=1, device_id=(part, lax.rem(me + step, group)), device_id_type=MESH
        )

    for step in range(1, parts):
        pl.semaphore_signal(
            barrier, inc=1, device_id=(lax.rem(part + step, parts), me), device_id_type=MESH
        )

    for load in loads:
        load.wait()
    mixed = (k_buf[...].astype(F32) * v_buf[...].astype(F32)).astype(BF16)
    grad_conv = (c_buf[...].astype(F32) * q_buf[...].astype(F32)).astype(BF16)
    spread = pick[...]

    def block(array, index):
        return array[:, index * group : (index + 1) * group]

    pairs = jnp.concatenate(
        [jnp.concatenate([block(mixed, i), block(grad_conv, i)], axis=1) for i in range(lanes)], axis=0
    )
    send_pair[...] = dot(spread, pairs, (1, 1)).astype(BF16).reshape(send_pair.shape)
    tap_rows = t_buf[...]
    tap_pairs = jnp.concatenate(
        [
            jnp.concatenate([block(tap_rows, 0), block(tap_rows, 1)], axis=1),
            jnp.concatenate([block(tap_rows, 2), jnp.zeros((rows, group), BF16)], axis=1),
        ],
        axis=0,
    )
    send_taps[...] = dot(spread, tap_pairs, (1, 1)).astype(BF16).reshape(send_taps.shape)
    recv_pair[me] = send_pair[me]
    recv_taps[me] = send_taps[me]

    pl.semaphore_wait(barrier, group - 1 + parts - 1)

    def exchange(source, target, index):
        @pl.loop(1, group)
        def _(step):
            peer = lax.rem(me + step, group)
            pltpu.make_async_remote_copy(
                src_ref=source.at[peer],
                dst_ref=target.at[me],
                send_sem=copy_sem.at[index, 0],
                recv_sem=copy_sem.at[index, 1],
                device_id=(part, peer),
                device_id_type=MESH,
            ).start()

    def arrived(buffer, index, count, side):
        some = buffer.at[pl.ds(0, count)]
        pltpu.make_async_copy(some, some, copy_sem.at[index, side]).wait()

    exchange(send_pair, recv_pair, 0)
    exchange(send_taps, recv_taps, 1)

    for table in tables:
        table.wait()

    def twist(real_part, imag_part, slot):
        rows_here = pl.ds(slot * group, group)
        cosines, sines = twist_cos[...], twist_sin[...]
        turned[rows_here, pl.ds(0, rows)] = (real_part * cosines + imag_part * sines).astype(BF16)
        turned[rows_here, pl.ds(rows, rows)] = (imag_part * cosines - real_part * sines).astype(BF16)

    def stage_forward(buffer, slots, first):
        partial = dot(forward[...], buffer[...].reshape(2 * group, buffer.shape[2]))
        for offset, (r, j) in enumerate(slots):
            real_part = partial[2 * r * group : (2 * r + 1) * group, j * rows : (j + 1) * rows]
            imag_part = partial[(2 * r + 1) * group : (2 * r + 2) * group, j * rows : (j + 1) * rows]
            twist(real_part, imag_part, first + offset)
        here = pl.ds(first * group, len(slots) * group)
        spectrum[here, :] = dot(turned[here, :], inner_forward[...])

    def halves(slot):
        here = pl.ds(slot * group, group)
        return spectrum[here, pl.ds(0, rows)], spectrum[here, pl.ds(rows, rows)]

    def multiply(left, right, conjugate, slot):
        left_real, left_imag = halves(left)
        right_real, right_imag = halves(right)
        if conjugate:
            right_imag = -right_imag
        here = pl.ds(slot * group, group)
        product[here, pl.ds(0, rows)] = (left_real * right_real - left_imag * right_imag).astype(BF16)
        product[here, pl.ds(rows, rows)] = (left_real * right_imag + left_imag * right_real).astype(BF16)

    def stage_inverse(slots, first, target):
        here = pl.ds(first * group, len(slots) * group)
        back = dot(product[here, :], inner_inverse[...])
        cosines, sines = twist_cos[...], twist_sin[...]
        for offset, (r, j) in enumerate(slots):
            real_part = back[offset * group : (offset + 1) * group, :rows]
            imag_part = back[offset * group : (offset + 1) * group, rows:]
            across = pl.ds(j * rows, rows)
            untwisted[pl.ds(2 * r * group, group), across] = (real_part * cosines - imag_part * sines).astype(BF16)
            untwisted[pl.ds((2 * r + 1) * group, group), across] = (real_part * sines + imag_part * cosines).astype(BF16)
        width = target.shape[2]
        target[...] = dot(inverse[...], untwisted[:, pl.ds(0, width)]).astype(BF16).reshape(target.shape)

    pair_slots = [(r, j) for r in range(2) for j in range(lanes)]
    tap_slots = [(0, 0), (1, 0), (0, 1)]

    arrived(recv_pair, 0, group - 1, 1)
    stage_forward(recv_pair, pair_slots, 0)
    for i in range(lanes):
        multiply(lanes + i, i, True, i)
    untwisted[pl.ds(2 * group, 2 * group), pl.ds(rows, rows)] = jnp.zeros((2 * group, rows), BF16)
    stage_inverse(tap_slots, 0, send_filter)
    share = group // parts

    def to_parts(source, target, index):
        for step in range(1, parts):
            peer = lax.rem(part + step, parts)
            pltpu.make_async_remote_copy(
                src_ref=source(peer),
                dst_ref=target,
                send_sem=copy_sem.at[index, 0],
                recv_sem=copy_sem.at[index, 1],
                device_id=(peer, me),
                device_id_type=MESH,
            ).start()

    to_parts(lambda peer: send_filter.at[pl.ds(peer * share, share)], recv_parts.at[part], 4)

    arrived(recv_taps, 1, group - 1, 1)
    stage_forward(recv_taps, tap_slots, 2 * lanes)
    for i in range(lanes):
        multiply(i, 2 * lanes + i, False, i)
        multiply(lanes + i, 2 * lanes + i, True, lanes + i)
    stage_inverse(pair_slots, 0, send_back)
    exchange(send_back, recv_back, 2)
    recv_back[me] = send_back[me]

    arrived(recv_parts, 4, parts - 1, 1)
    total = send_filter[pl.ds(part * share, share)].astype(F32)
    for step in range(1, parts):
        total = total + recv_parts[lax.rem(part + step, parts)].astype(F32)
    mine = sum_filter.at[pl.ds(part * share, share)]
    mine[...] = total.astype(BF16)
    to_parts(lambda peer: mine, mine, 5)
    arrived(sum_filter, 5, (parts - 1) * share, 1)
    exchange(sum_filter, recv_filter, 3)
    recv_filter[me] = sum_filter[me]

    arrived(recv_back, 2, group - 1, 1)
    flat = recv_back[...].reshape(2 * group, lanes * rows)
    for i in range(lanes):
        both = dot(flat[:, i * rows : (i + 1) * rows], spread, (0, 0))
        conv, grad_mixed = both[:, :group], both[:, group:]
        here = pl.ds(i * group, group)
        gated[:, here] = (q_buf[:, here].astype(F32) * conv).astype(BF16)
        grad_queries[:, here] = (c_buf[:, here].astype(F32) * conv).astype(BF16)
        grad_keys[:, here] = (v_buf[:, here].astype(F32) * grad_mixed).astype(BF16)
        grad_values[:, here] = (k_buf[:, here].astype(F32) * grad_mixed).astype(BF16)
    arrived(recv_filter, 3, group - 1, 1)
    flat = recv_filter[...].reshape(2 * group, 2 * rows)
    for r, j in tap_slots:
        if r == 0:
            both = dot(flat[:, j * rows : (j + 1) * rows], spread, (0, 0))
        filter_grad[:, pl.ds((2 * j + r) * group, group)] = both[:, r * group : (r + 1) * group]

    for index, buffer in enumerate([send_pair, send_taps, send_back, sum_filter]):
        arrived(buffer, index, group - 1, 0)
    arrived(recv_parts, 4, parts - 1, 0)
    arrived(sum_filter, 5, (parts - 1) * share, 0)


def shards(group, parts, queries, keys, values, filter_taps, cotangent):
    rows, channels = filter_taps.shape
    lanes = channels // group
    tables = constant_tables(group, rows)
    share = group // parts
    vmem = pltpu.VMEM
    local = (rows, channels)
    pair = (group, 2, lanes * rows)
    single = (group, 2, 2 * rows)
    outs = pl.pallas_call(
        functools.partial(kernel, group, parts),
        out_shape=[jax.ShapeDtypeStruct(local, BF16)] * 4 + [jax.ShapeDtypeStruct(local, F32)],
        in_specs=[pl.BlockSpec(memory_space=pl.ANY)] * 12,
        out_specs=[pl.BlockSpec(memory_space=vmem)] * 5,
        scratch_shapes=[vmem(local, BF16)] * 5
        + [vmem(table.shape, table.dtype) for table in tables]
        + [vmem(pair, BF16)] * 2
        + [vmem(single, BF16)] * 2
        + [vmem(pair, BF16)] * 2
        + [vmem(single, BF16)] * 3
        + [
            vmem((parts, share, 2, 2 * rows), BF16),
            vmem((3 * lanes * group, 2 * rows), BF16),
            vmem((3 * lanes * group, 2 * rows), F32),
            vmem((2 * lanes * group, 2 * rows), BF16),
            vmem((4 * group, lanes * rows), BF16),
            pltpu.SemaphoreType.DMA((6,)),
            pltpu.SemaphoreType.DMA((6,)),
            pltpu.SemaphoreType.DMA((6, 2)),
        ],
        compiler_params=pltpu.CompilerParams(
            collective_id=0, has_side_effects=True, vmem_limit_bytes=56 << 20
        ),
    )(queries[0], keys[0], values[0], filter_taps, cotangent[0], *tables)
    return tuple(out[None] for out in outs[:4]) + (outs[4],)


def solution(mesh):
    spec = P("dp", "ctx", None)
    return jax.shard_map(
        functools.partial(shards, mesh.shape["ctx"], mesh.shape["dp"]),
        mesh=mesh,
        in_specs=(spec, spec, spec, P("ctx", None), spec),
        out_specs=(spec, spec, spec, spec, P("ctx", None)),
        check_vma=False,
    )
```

profile of v0, /device:TPU:1, one launch (start us, length us, event | category | flops | bytes accessed | tf_op | source)
XLA Modules:
  0.0 57.7 jit_solution(7581163808621946342)
XLA Ops:
  0.6 52.5 %shard_map.155 = (bf16[128,384]{1,0:T(8,128)(2,1)}, bf16[128,384]{1,0:T(8,128)(2,1)}, bf16[128,384]{1,0:T(8,128)(2,1)}, bf16[128,384]{1,0:T(8,128)(2,1)}, f32[128,384]{1,0:T(8,128)}) custom-call(bf16[128,384]{1,0:T(8,128)(2,1)} %bitcast.8, bf16[128,384]{1,0:T(8,128)(2,1)} %bitcast.9, bf16[128,384]{1,0:T(8,128)(2,1)} %bitcast.10, bf16[128,384]{1,0:T(8,128)(2,1)} %taps.1, ...), custom_call_target="tpu_custom_call" | custom-call | tf_op jit(solution)/shard_map/pallas_call | solution.py:312
  53.2 0.0 copy-start.3
  53.2 1.6 %copy.22 = bf16[1,128,384]{2,1,0:T(8,128)(2,1)} copy(bf16[1,128,384]{2,1,0:T(8,128)(2,1)} %bitcast.15) | data formatting | bytes 196608
  54.8 0.0 copy-done.3
  54.8 0.0 copy-start.2
  54.8 0.0 copy-start.1
  54.8 0.6 %copy.23 = bf16[1,128,384]{2,1,0:T(8,128)(2,1)} copy(bf16[1,128,384]{2,1,0:T(8,128)(2,1)S(1)} %bitcast.14) | data formatting | bytes 196608
  55.4 0.3 copy-done.2
  55.7 0.0 copy-start
  55.7 0.6 %copy.24 = bf16[1,128,384]{2,1,0:T(8,128)(2,1)} copy(bf16[1,128,384]{2,1,0:T(8,128)(2,1)S(1)} %bitcast.13) | data formatting | bytes 196608
  56.4 0.0 copy-done.1
  56.4 0.6 %copy.25 = bf16[1,128,384]{2,1,0:T(8,128)(2,1)} copy(bf16[1,128,384]{2,1,0:T(8,128)(2,1)S(1)} %bitcast.12) | data formatting | bytes 196608
  57.0 0.0 copy-done
  57.0 0.7 %copy.26 = f32[128,384]{1,0:T(8,128)} copy(f32[128,384]{1,0:T(8,128)S(1)} %copy-done) | data formatting | bytes 393216
Async XLA Ops:
  53.2 1.6 %copy-start.3 = (bf16[128,384]{1,0:T(8,128)(2,1)S(1)}, bf16[128,384]{1,0:T(8,128)(2,1)}, u32[]{:S(2)}) copy-start(bf16[128,384]{1,0:T(8,128)(2,1)} %get-tuple-element.11) | copy-start | bytes 294916
  54.8 0.9 %copy-start.2 = (bf16[128,384]{1,0:T(8,128)(2,1)S(1)}, bf16[128,384]{1,0:T(8,128)(2,1)}, u32[]{:S(2)}) copy-start(bf16[128,384]{1,0:T(8,128)(2,1)} %get-tuple-element.12) | copy-start | bytes 294916
  54.8 1.6 %copy-start.1 = (bf16[128,384]{1,0:T(8,128)(2,1)S(1)}, bf16[128,384]{1,0:T(8,128)(2,1)}, u32[]{:S(2)}) copy-start(bf16[128,384]{1,0:T(8,128)(2,1)} %get-tuple-element.13) | copy-start | bytes 294916
  55.7 1.3 %copy-start = (f32[128,384]{1,0:T(8,128)S(1)}, f32[128,384]{1,0:T(8,128)}, u32[]{:S(2)}) copy-start(f32[128,384]{1,0:T(8,128)} %get-tuple-element.24) | copy-start | bytes 589828
where the time goes:
time: 57.9 us; the launch traced here: 57.7 us
  Pallas kernels  52.5 us (91%)
  local copies, waits for them, and re-layouts  4.47 us (8%)
  between operations  0.65 us (1%)
    pallas_call x1, Pallas kernels, shards(): pl.pallas_call(functools.partial(kernel, group, parts), out_shape=[jax.Sh...  52.5 us
    unnamed x13, local copies, waits for them, and re-layouts  4.47 us

commit v1 on v0

--- a/solution.py
+++ b/solution.py
@@ -66,11 +66,8 @@
     pick_hbm,
     twist_cos_hbm,
     twist_sin_hbm,
-    gated,
-    grad_queries,
-    grad_keys,
-    grad_values,
-    filter_grad,
+    recv_back,
+    all_filter,
     q_buf,
     k_buf,
     v_buf,
@@ -88,11 +85,10 @@
     send_taps,
     recv_taps,
     send_back,
-    recv_back,
     send_filter,
+    part_filter,
     sum_filter,
     recv_filter,
-    recv_parts,
     turned,
     spectrum,
     product,
@@ -100,9 +96,16 @@
     in_sem,
     table_sem,
     copy_sem,
+    core_sem,
+    ready_sem,
 ):
     me = lax.axis_index("ctx")
     part = lax.axis_index("dp")
+    core = lax.rem(part, 2)
+    pair = part // 2
+    other = pair * 2 + 1 - core
+    half = group // 2
+    my_half = me // half
     lanes = queries.shape[1] // group
     rows = queries.shape[0]
 
@@ -164,9 +167,15 @@
     )
     send_taps[...] = dot(spread, tap_pairs, (1, 1)).astype(BF16).reshape(send_taps.shape)
     recv_pair[me] = send_pair[me]
-    recv_taps[me] = send_taps[me]
 
     pl.semaphore_wait(barrier, group - 1 + parts - 1)
+    for step in range(1, parts):
+        pl.semaphore_signal(
+            ready_sem.at[step],
+            inc=1,
+            device_id=(lax.rem(part + step, parts), me),
+            device_id_type=MESH,
+        )
 
     def exchange(source, target, index):
         @pl.loop(1, group)
@@ -186,7 +195,33 @@
         pltpu.make_async_copy(some, some, copy_sem.at[index, side]).wait()
 
     exchange(send_pair, recv_pair, 0)
-    exchange(send_taps, recv_taps, 1)
+
+    for step in range(1, parts):
+        pl.semaphore_wait(ready_sem.at[step], 1)
+
+    @pl.loop(0, half)
+    def _(step):
+        peer = half * (1 - core) + lax.rem(me + step, half)
+        pltpu.make_async_remote_copy(
+            src_ref=send_taps.at[peer],
+            dst_ref=recv_taps.at[me],
+            send_sem=copy_sem.at[1, 0],
+            recv_sem=copy_sem.at[1, 1],
+            device_id=(pair * 2 + my_half, peer),
+            device_id_type=MESH,
+        ).start()
+
+    def to_core(source, target, index):
+        copy = pltpu.make_async_remote_copy(
+            src_ref=source,
+            dst_ref=target,
+            send_sem=core_sem.at[index, 0],
+            recv_sem=core_sem.at[index, 1],
+            device_id=(other, me),
+            device_id_type=MESH,
+        )
+        copy.start()
+        return copy
 
     for table in tables:
         table.wait()
@@ -235,29 +270,19 @@
     pair_slots = [(r, j) for r in range(2) for j in range(lanes)]
     tap_slots = [(0, 0), (1, 0), (0, 1)]
 
+    arrived(recv_taps, 1, half, 1)
+    got = recv_taps.at[pl.ds(half * core, half)]
+    taps_copy = to_core(got, got, 0)
+
     arrived(recv_pair, 0, group - 1, 1)
     stage_forward(recv_pair, pair_slots, 0)
     for i in range(lanes):
         multiply(lanes + i, i, True, i)
     untwisted[pl.ds(2 * group, 2 * group), pl.ds(rows, rows)] = jnp.zeros((2 * group, rows), BF16)
     stage_inverse(tap_slots, 0, send_filter)
-    share = group // parts
-
-    def to_parts(source, target, index):
-        for step in range(1, parts):
-            peer = lax.rem(part + step, parts)
-            pltpu.make_async_remote_copy(
-                src_ref=source(peer),
-                dst_ref=target,
-                send_sem=copy_sem.at[index, 0],
-                recv_sem=copy_sem.at[index, 1],
-                device_id=(peer, me),
-                device_id_type=MESH,
-            ).start()
-
-    to_parts(lambda peer: send_filter.at[pl.ds(peer * share, share)], recv_parts.at[part], 4)
-
-    arrived(recv_taps, 1, group - 1, 1)
+    filter_copy = to_core(send_filter.at[pl.ds(half * core, half)], part_filter, 1)
+
+    taps_copy.wait_recv()
     stage_forward(recv_taps, tap_slots, 2 * lanes)
     for i in range(lanes):
         multiply(i, 2 * lanes + i, False, i)
@@ -266,74 +291,119 @@
     exchange(send_back, recv_back, 2)
     recv_back[me] = send_back[me]
 
-    arrived(recv_parts, 4, parts - 1, 1)
-    total = send_filter[pl.ds(part * share, share)].astype(F32)
-    for step in range(1, parts):
-        total = total + recv_parts[lax.rem(part + step, parts)].astype(F32)
-    mine = sum_filter.at[pl.ds(part * share, share)]
+    filter_copy.wait_recv()
+    kept = half * (1 - core)
+    sum_filter[...] = (send_filter[pl.ds(kept, half)].astype(F32) + part_filter[...].astype(F32)).astype(BF16)
+    for to_pair in range(parts // 2):
+
+        @pl.loop(0, half)
+        def _(step):
+            peer = lax.rem(me + step, half)
+            pltpu.make_async_remote_copy(
+                src_ref=sum_filter.at[peer],
+                dst_ref=recv_filter.at[pair, lax.rem(me, half)],
+                send_sem=copy_sem.at[3, 0],
+                recv_sem=copy_sem.at[3, 1],
+                device_id=(to_pair * 2 + my_half, kept + peer),
+                device_id_type=MESH,
+            ).start()
+
+    pltpu.make_async_copy(recv_filter, recv_filter, copy_sem.at[3, 1]).wait()
+    total = recv_filter[0].astype(F32)
+    for index in range(1, parts // 2):
+        total = total + recv_filter[index].astype(F32)
+    mine = all_filter.at[pl.ds(half * core, half)]
     mine[...] = total.astype(BF16)
-    to_parts(lambda peer: mine, mine, 5)
-    arrived(sum_filter, 5, (parts - 1) * share, 1)
-    exchange(sum_filter, recv_filter, 3)
-    recv_filter[me] = sum_filter[me]
+    all_copy = to_core(mine, mine, 2)
 
     arrived(recv_back, 2, group - 1, 1)
-    flat = recv_back[...].reshape(2 * group, lanes * rows)
+    all_copy.wait_recv()
+    arrived(send_pair, 0, group - 1, 0)
+    arrived(send_taps, 1, half, 0)
+    arrived(send_back, 2, group - 1, 0)
+    pltpu.make_async_copy(recv_filter, recv_filter, copy_sem.at[3, 0]).wait()
+    for copy in (taps_copy, filter_copy, all_copy):
+        copy.wait_send()
+
+
+def finish(
+    group,
+    queries,
+    keys,
+    values,
+    cotangent,
+    back,
+    taps_back,
+    pick,
+    gated,
+    grad_queries,
+    grad_keys,
+    grad_values,
+    filter_grad,
+):
+    rows, channels = queries.shape
+    lanes = channels // group
+    spread = pick[...]
+    flat = back[...].reshape(2 * group, lanes * rows)
     for i in range(lanes):
         both = dot(flat[:, i * rows : (i + 1) * rows], spread, (0, 0))
         conv, grad_mixed = both[:, :group], both[:, group:]
         here = pl.ds(i * group, group)
-        gated[:, here] = (q_buf[:, here].astype(F32) * conv).astype(BF16)
-        grad_queries[:, here] = (c_buf[:, here].astype(F32) * conv).astype(BF16)
-        grad_keys[:, here] = (v_buf[:, here].astype(F32) * grad_mixed).astype(BF16)
-        grad_values[:, here] = (k_buf[:, here].astype(F32) * grad_mixed).astype(BF16)
-    arrived(recv_filter, 3, group - 1, 1)
-    flat = recv_filter[...].reshape(2 * group, 2 * rows)
-    for r, j in tap_slots:
-        if r == 0:
-            both = dot(flat[:, j * rows : (j + 1) * rows], spread, (0, 0))
-        filter_grad[:, pl.ds((2 * j + r) * group, group)] = both[:, r * group : (r + 1) * group]
-
-    for index, buffer in enumerate([send_pair, send_taps, send_back, sum_filter]):
-        arrived(buffer, index, group - 1, 0)
-    arrived(recv_parts, 4, parts - 1, 0)
-    arrived(sum_filter, 5, (parts - 1) * share, 0)
+        gated[:, here] = (queries[:, here].astype(F32) * conv).astype(BF16)
+        grad_queries[:, here] = (cotangent[:, here].astype(F32) * conv).astype(BF16)
+        grad_keys[:, here] = (values[:, here].astype(F32) * grad_mixed).astype(BF16)
+        grad_values[:, here] = (keys[:, here].astype(F32) * grad_mixed).astype(BF16)
+    flat = taps_back[...].reshape(2 * group, 2 * rows)
+    first = dot(flat[:, :rows], spread, (0, 0))
+    filter_grad[:, pl.ds(0, 2 * group)] = first
+    filter_grad[:, pl.ds(2 * group, group)] = dot(flat[:, rows:], spread, (0, 0))[:, :group]
 
 
 def shards(group, parts, queries, keys, values, filter_taps, cotangent):
     rows, channels = filter_taps.shape
     lanes = channels // group
     tables = constant_tables(group, rows)
-    share = group // parts
     vmem = pltpu.VMEM
     local = (rows, channels)
     pair = (group, 2, lanes * rows)
     single = (group, 2, 2 * rows)
-    outs = pl.pallas_call(
+    half = group // 2
+    arrays = (queries[0], keys[0], values[0], filter_taps, cotangent[0])
+    back, taps_back = pl.pallas_call(
         functools.partial(kernel, group, parts),
-        out_shape=[jax.ShapeDtypeStruct(local, BF16)] * 4 + [jax.ShapeDtypeStruct(local, F32)],
+        out_shape=[jax.ShapeDtypeStruct(pair, BF16), jax.ShapeDtypeStruct(single, BF16)],
         in_specs=[pl.BlockSpec(memory_space=pl.ANY)] * 12,
-        out_specs=[pl.BlockSpec(memory_space=vmem)] * 5,
+        out_specs=[pl.BlockSpec(memory_space=vmem)] * 2,
         scratch_shapes=[vmem(local, BF16)] * 5
         + [vmem(table.shape, table.dtype) for table in tables]
         + [vmem(pair, BF16)] * 2
         + [vmem(single, BF16)] * 2
-        + [vmem(pair, BF16)] * 2
-        + [vmem(single, BF16)] * 3
+        + [vmem(pair, BF16)]
+        + [vmem(single, BF16)]
+        + [vmem((half,) + single[1:], BF16)] * 2
         + [
-            vmem((parts, share, 2, 2 * rows), BF16),
+            vmem((parts // 2, half) + single[1:], BF16),
             vmem((3 * lanes * group, 2 * rows), BF16),
             vmem((3 * lanes * group, 2 * rows), F32),
             vmem((2 * lanes * group, 2 * rows), BF16),
             vmem((4 * group, lanes * rows), BF16),
             pltpu.SemaphoreType.DMA((6,)),
             pltpu.SemaphoreType.DMA((6,)),
-            pltpu.SemaphoreType.DMA((6, 2)),
+            pltpu.SemaphoreType.DMA((4, 2)),
+            pltpu.SemaphoreType.DMA((3, 2)),
+            pltpu.SemaphoreType.REGULAR((parts,)),
         ],
         compiler_params=pltpu.CompilerParams(
-            collective_id=0, has_side_effects=True, vmem_limit_bytes=56 << 20
+            collective_id=0, has_side_effects=True, vmem_limit_bytes=60 << 20
         ),
-    )(queries[0], keys[0], values[0], filter_taps, cotangent[0], *tables)
+    )(*arrays, *tables)
+    outs = pl.pallas_call(
+        functools.partial(finish, group),
+        out_shape=[jax.ShapeDtypeStruct(local, BF16)] * 4 + [jax.ShapeDtypeStruct(local, F32)],
+        in_specs=[pl.BlockSpec(memory_space=vmem)] * 7,
+        out_specs=[pl.BlockSpec(memory_space=vmem)] * 5,
+        compiler_params=pltpu.CompilerParams(vmem_limit_bytes=60 << 20),
+    )(queries[0], keys[0], values[0], cotangent[0], back, taps_back, tables[4])
     return tuple(out[None] for out in outs[:4]) + (outs[4],)
 
 

time: 57.9 us -> 48.6 us (0.84)
  Pallas kernels: 52.5 us -> 47.5 us
  local copies, waits for them, and re-layouts: 4.47 us -> 0 us
    pallas_call x1, Pallas kernels: 52.5 us -> 45.1 us  [shards(): pl.pallas_call(functools.partial(kernel, group, parts), out_shape=[jax.Sh...]
    unnamed x13 -> x0, local copies, waits for them, and re-layouts: 4.47 us -> none
    pallas_call x0 -> x1, Pallas kernels: none -> 2.33 us  [shards(): pl.pallas_call(functools.partial(finish, group), out_shape=[jax.ShapeDtyp...]
where the time goes in v1:
time: 48.6 us; the launch traced here: 48.1 us
  Pallas kernels  47.5 us (98%)
  between operations  0.64 us (1%)
    pallas_call x1, Pallas kernels, shards(): pl.pallas_call(functools.partial(kernel, group, parts), out_shape=[jax.Sh...  45.1 us
    pallas_call x1, Pallas kernels, shards(): pl.pallas_call(functools.partial(finish, group), out_shape=[jax.ShapeDtyp...  2.33 us

profile of v1, /device:TPU:1, one launch (start us, length us, event | category | flops | bytes accessed | tf_op | source)
XLA Modules:
  0.0 48.1 jit_solution(4342784831453688452)
XLA Ops:
  0.6 45.1 %shard_map.155 = (bf16[128,2,384]{2,1,0:T(2,128)(2,1)}, bf16[128,2,256]{2,1,0:T(2,128)(2,1)}) custom-call(bf16[128,384]{1,0:T(8,128)(2,1)} %bitcast.8, bf16[128,384]{1,0:T(8,128)(2,1)} %bitcast.10, bf16[128,384]{1,0:T(8,128)(2,1)} %bitcast.12, bf16[128,384]{1,0:T(8,128)(2,1)} %taps.1, bf16[128,384]{1,0:T(8,128)(2,1)} %bitcast.14, ...), custom_call_target="tpu_custom_call" | custom-call | tf_op jit(solution)/shard_map/pallas_call | solution.py:372
  45.8 2.3 %shard_map.156 = (bf16[128,384]{1,0:T(8,128)(2,1)}, bf16[128,384]{1,0:T(8,128)(2,1)}, bf16[128,384]{1,0:T(8,128)(2,1)}, bf16[128,384]{1,0:T(8,128)(2,1)}, f32[128,384]{1,0:T(8,128)}) custom-call(bf16[128,384]{1,0:T(8,128)(2,1)} %bitcast.9, bf16[128,384]{1,0:T(8,128)(2,1)} %bitcast.11, bf16[128,384]{1,0:T(8,128)(2,1)} %bitcast.13, bf16[128,384]{1,0:T(8,128)(2,1)} %bitcast.15, ...), custom_call_target="tpu_custom_call" | custom-call | tf_op jit(solution)/shard_map/pallas_call | solution.py:400

commit v2 on v1

v2 whole, which is shorter than its diff:
```python
import functools

import jax
import jax.numpy as jnp
import numpy as np
from jax import lax
from jax.experimental import pallas as pl
from jax.experimental.pallas import tpu as pltpu
from jax.sharding import PartitionSpec as P

MESH = pl.DeviceIdType.MESH
BF16 = jnp.bfloat16
F32 = jnp.float32


def dot(left, right, contract=(1, 0)):
    dims = (((contract[0],), (contract[1],)), ((), ()))
    return lax.dot_general(left, right, dims, preferred_element_type=F32)


def constant_tables(group, rows):
    total = group * rows
    outer = np.arange(group)
    inner = np.arange(rows)
    angle_outer = 2 * np.pi * np.outer(outer + 0.25, outer) / group
    angle_twist = 2 * np.pi * np.outer(outer + 0.25, inner) / total
    angle_inner = 2 * np.pi * np.outer(inner, inner) / rows
    cos_outer, sin_outer = np.cos(angle_outer), np.sin(angle_outer)
    forward = np.zeros((2, 2, group, group, 2))
    inverse = np.zeros((group, 2, 2, 2, group))
    scale = 1.0 / (total * np.sqrt(total))
    for slot in range(2):
        forward[slot, 0, :, :, slot] = cos_outer
        forward[slot, 1, :, :, slot] = -sin_outer
        inverse[:, slot, slot, 0, :] = cos_outer.T * scale
        inverse[:, slot, slot, 1, :] = -sin_outer.T * scale
    cos_inner, sin_inner = np.cos(angle_inner), np.sin(angle_inner)
    inner_forward = np.block([[cos_inner, -sin_inner], [sin_inner, cos_inner]])
    inner_inverse = np.block([[cos_inner, sin_inner], [-sin_inner, cos_inner]])
    pick = np.zeros((group, 2, 2, group))
    for slot in range(2):
        pick[outer, slot, slot, outer] = 1.0
    return (
        jnp.asarray(forward.reshape(4 * group, 2 * group), BF16),
        jnp.asarray(inverse.reshape(2 * group, 4 * group), BF16),
        jnp.asarray(inner_forward, BF16),
        jnp.asarray(inner_inverse, BF16),
        jnp.asarray(pick.reshape(2 * group, 2 * group), BF16),
        jnp.asarray(np.cos(angle_twist), F32),
        jnp.asarray(np.sin(angle_twist), F32),
    )


GRID = (8, 4, 4)


def far_first(count, step):
    return count // 2 + (step + 1) // 2 * (1 - 2 * (step % 2))


def planes(me):
    _, wide, deep = GRID
    x, z = lax.rem(me // deep, wide), lax.rem(me, deep)
    xs = [lax.rem(x + far_first(wide, step), wide) * deep for step in range(wide)]
    zs = [lax.rem(z + far_first(deep, step), deep) for step in range(deep)]
    return [one + two for one in xs for two in zs]


def others(me, act, steps, own_row):
    rows, wide, deep = GRID
    y = me // (wide * deep)
    plane = planes(me)

    @pl.loop(steps[0], steps[1])
    def _(step):
        offset = rows // 2 + (step + 1) // 2 * (1 - 2 * lax.rem(step, 2))
        act(lax.rem(y + offset, rows), plane)

    if own_row:
        act(y, plane[:-1])


def kernel(
    group,
    parts,
    queries,
    keys,
    values,
    taps,
    cotangent,
    forward_hbm,
    inverse_hbm,
    inner_forward_hbm,
    inner_inverse_hbm,
    pick_hbm,
    twist_cos_hbm,
    twist_sin_hbm,
    recv_back,
    q_buf,
    k_buf,
    v_buf,
    t_buf,
    c_buf,
    forward,
    inverse,
    inner_forward,
    inner_inverse,
    pick,
    twist_cos,
    twist_sin,
    send_there,
    recv_there,
    send_back,
    send_filter,
    part_filter,
    cross_filter,
    turned,
    spectrum,
    product,
    untwisted,
    in_sem,
    table_sem,
    copy_sem,
    core_sem,
    ready_sem,
):
    me = lax.axis_index("ctx")
    part = lax.axis_index("dp")
    core = lax.rem(part, 2)
    pair = part // 2
    twin = pair * 2 + 1 - core
    half = group // 2
    rows_all, wide, deep = GRID
    plane = wide * deep
    mine = lax.rem(me // half + core, 2)
    theirs = 1 - mine
    mate = lax.rem(pair + 1, parts // 2) * 2 + core
    lanes = queries.shape[1] // group
    rows = queries.shape[0]

    barrier = pltpu.get_barrier_semaphore()

    def greet(row, places):
        for place in places:
            pl.semaphore_signal(
                barrier, inc=1, device_id=(part, row * plane + place), device_id_type=MESH
            )

    pl.semaphore_signal(barrier, inc=1, device_id=(mate, me), device_id_type=MESH)
    others(me, greet, (0, rows_all - 1), True)
    pl.semaphore_signal(barrier, inc=1, device_id=(twin, me), device_id_type=MESH)

    loads = [
        pltpu.make_async_copy(source, target, in_sem.at[index])
        for index, (source, target) in enumerate(
            [(keys, k_buf), (values, v_buf), (queries, q_buf), (cotangent, c_buf), (taps, t_buf), (pick_hbm, pick)]
        )
    ]
    tables = [
        pltpu.make_async_copy(source, target, table_sem.at[index])
        for index, (source, target) in enumerate(
            [
                (forward_hbm, forward),
                (twist_cos_hbm, twist_cos),
                (twist_sin_hbm, twist_sin),
                (inner_forward_hbm, inner_forward),
                (inner_inverse_hbm, inner_inverse),
                (inverse_hbm, inverse),
            ]
        )
    ]
    for load in loads + tables:
        load.start()

    for load in loads:
        load.wait()

    def keep_own(source, target):
        here = pl.ds(0, lanes * rows)
        target[me, :, here] = source[me, :, here]

        @pl.when(core == 0)
        def _():
            here = pl.ds(lanes * rows, 2 * rows)
            target[me, :, here] = source[me, :, here]

    mixed = (k_buf[...].astype(F32) * v_buf[...].astype(F32)).astype(BF16)
    grad_conv = (c_buf[...].astype(F32) * q_buf[...].astype(F32)).astype(BF16)
    spread = pick[...]

    def block(array, index):
        return array[:, index * group : (index + 1) * group]

    pairs = jnp.concatenate(
        [jnp.concatenate([block(mixed, i), block(grad_conv, i)], axis=1) for i in range(lanes)], axis=0
    )
    width = lanes * rows
    there = dot(spread, pairs, (1, 1)).astype(BF16)
    send_there[:, :, pl.ds(0, width)] = there.reshape(group, 2, width)
    tap_rows = t_buf[...]
    tap_pairs = jnp.concatenate(
        [
            jnp.concatenate([block(tap_rows, 0), block(tap_rows, 1)], axis=1),
            jnp.concatenate([block(tap_rows, 2), jnp.zeros((rows, group), BF16)], axis=1),
        ],
        axis=0,
    )
    there = dot(spread, tap_pairs, (1, 1)).astype(BF16)
    send_there[:, :, pl.ds(width, 2 * rows)] = there.reshape(group, 2, 2 * rows)
    keep_own(send_there, recv_there)

    pl.semaphore_wait(barrier, group - 1 + 2)
    pl.semaphore_signal(ready_sem, inc=1, device_id=(mate, me), device_id_type=MESH)

    def remote(source, target, peer_part, peer, index):
        return pltpu.make_async_remote_copy(
            src_ref=source,
            dst_ref=target,
            send_sem=copy_sem.at[index, 0],
            recv_sem=copy_sem.at[index, 1],
            device_id=(peer_part, peer),
            device_id_type=MESH,
        )

    def exchange(source, target, index, steps, own_row):
        def send(row, places):
            whole = row // (rows_all // 2) == mine

            @pl.when(whole)
            def _():
                for place in places:
                    peer = row * plane + place
                    remote(source.at[peer], target.at[me], part, peer, index).start()

            @pl.when(jnp.logical_not(whole))
            def _():
                here = pl.ds(0, width)
                for place in places:
                    peer = row * plane + place
                    remote(source.at[peer, :, here], target.at[me, :, here], part, peer, index + 1).start()

        others(me, send, steps, own_row)

    def wait_bytes(some, sem):
        pltpu.make_async_copy(some, some, sem).wait()

    def finished(buffer, index, side):
        for value in range(2):

            @pl.when(core == value)
            def _():
                wait_bytes(buffer.at[pl.ds(0, half - 1 + value)], copy_sem.at[index, side])
                wait_bytes(buffer.at[pl.ds(0, half - value), :, pl.ds(0, width)], copy_sem.at[index + 1, side])

    first, rest = pl.ds(0, width), pl.ds(width, 2 * rows)

    def send_first(row, places):
        for place in places:
            peer = row * plane + place
            remote(send_there.at[peer, :, first], recv_there.at[me, :, first], part, peer, 0).start()

    def send_rest(row, places):
        @pl.when(row // (rows_all // 2) == mine)
        def _():
            for place in places:
                peer = row * plane + place
                remote(send_there.at[peer, :, rest], recv_there.at[me, :, rest], part, peer, 1).start()

    others(me, send_first, (0, rows_all - 1), True)
    others(me, send_rest, (0, rows_all - 1), True)

    def finished_first(side):
        wait_bytes(recv_there.at[pl.ds(0, group - 1), :, first], copy_sem.at[0, side])

    def finished_rest(side):
        for value in range(2):

            @pl.when(core == value)
            def _():
                wait_bytes(recv_there.at[pl.ds(0, half - 1 + value), :, rest], copy_sem.at[1, side])


    def to_core(source, target, index):
        return pltpu.make_async_remote_copy(
            src_ref=source,
            dst_ref=target,
            send_sem=core_sem.at[index, 0],
            recv_sem=core_sem.at[index, 1],
            device_id=(twin, me),
            device_id_type=MESH,
        )

    def second(buffer, which):
        return buffer.at[pl.ds(which * half, half), :, pl.ds(width, 2 * rows)]

    for table in tables:
        table.wait()

    def twist(real_part, imag_part, slot):
        rows_here = pl.ds(slot * group, group)
        cosines, sines = twist_cos[...], twist_sin[...]
        turned[rows_here, pl.ds(0, rows)] = (real_part * cosines + imag_part * sines).astype(BF16)
        turned[rows_here, pl.ds(rows, rows)] = (imag_part * cosines - real_part * sines).astype(BF16)

    def stage_forward(buffer, slots, first):
        partial = dot(forward[...], buffer.reshape(2 * group, buffer.shape[2]))
        for offset, (r, j) in enumerate(slots):
            real_part = partial[2 * r * group : (2 * r + 1) * group, j * rows : (j + 1) * rows]
            imag_part = partial[(2 * r + 1) * group : (2 * r + 2) * group, j * rows : (j + 1) * rows]
            twist(real_part, imag_part, first + offset)
        here = pl.ds(first * group, len(slots) * group)
        spectrum[here, :] = dot(turned[here, :], inner_forward[...])

    def halves(slot):
        here = pl.ds(slot * group, group)
        return spectrum[here, pl.ds(0, rows)], spectrum[here, pl.ds(rows, rows)]

    def multiply(left, right, conjugate, slot):
        left_real, left_imag = halves(left)
        right_real, right_imag = halves(right)
        if conjugate:
            right_imag = -right_imag
        here = pl.ds(slot * group, group)
        product[here, pl.ds(0, rows)] = (left_real * right_real - left_imag * right_imag).astype(BF16)
        product[here, pl.ds(rows, rows)] = (left_real * right_imag + left_imag * right_real).astype(BF16)

    def stage_inverse(slots, first, target):
        here = pl.ds(first * group, len(slots) * group)
        back = dot(product[here, :], inner_inverse[...])
        cosines, sines = twist_cos[...], twist_sin[...]
        for offset, (r, j) in enumerate(slots):
            real_part = back[offset * group : (offset + 1) * group, :rows]
            imag_part = back[offset * group : (offset + 1) * group, rows:]
            across = pl.ds(j * rows, rows)
            untwisted[pl.ds(2 * r * group, group), across] = (real_part * cosines - imag_part * sines).astype(BF16)
            untwisted[pl.ds((2 * r + 1) * group, group), across] = (real_part * sines + imag_part * cosines).astype(BF16)
        size = (slots[-1][1] + 1) * rows
        back = dot(inverse[...], untwisted[:, pl.ds(0, size)]).astype(BF16)
        target[:, :, pl.ds(0, size)] = back.reshape(group, 2, size)

    pair_slots = [(r, j) for r in range(2) for j in range(lanes)]
    tap_slots = [(0, 0), (1, 0), (0, 1)]

    finished_first(1)
    stage_forward(recv_there[:, :, first], pair_slots, 0)
    for i in range(lanes):
        multiply(lanes + i, i, True, i)
    untwisted[pl.ds(2 * group, 2 * group), pl.ds(rows, rows)] = jnp.zeros((2 * group, rows), BF16)
    stage_inverse(tap_slots, 0, send_filter)
    filter_copy = to_core(send_filter.at[pl.ds(theirs * half, half)], part_filter, 1)
    filter_copy.start()
    finished_rest(1)
    taps_copy = to_core(second(recv_there, mine), second(recv_there, mine), 0)
    taps_copy.start()

    filter_copy.wait_recv()
    both = send_filter[pl.ds(mine * half, half)].astype(F32) + part_filter[...].astype(F32)
    send_back[pl.ds(mine * half, half), :, rest] = both.astype(BF16)
    pl.semaphore_wait(ready_sem, 1)

    def cross(row, places):
        @pl.when(row // (rows_all // 2) == mine)
        def _():
            for place in places:
                peer = row * plane + place
                remote(
                    send_back.at[peer, :, rest], cross_filter.at[lax.rem(me, half)], mate, peer, 4
                ).start()

    others(me, cross, (0, rows_all), False)

    taps_copy.wait_recv()
    stage_forward(recv_there[:, :, rest], tap_slots, 2 * lanes)
    for i in range(lanes):
        multiply(i, 2 * lanes + i, False, i)
        multiply(lanes + i, 2 * lanes + i, True, lanes + i)
    stage_inverse(pair_slots, 0, send_back)
    keep_own(send_back, recv_back)
    exchange(send_back, recv_back, 2, (0, rows_all - 1), True)

    finished(recv_back, 2, 1)
    wait_bytes(cross_filter, copy_sem.at[4, 1])
    here = second(recv_back, mine)
    here[...] = (here[...].astype(F32) + cross_filter[...].astype(F32)).astype(BF16)
    all_copy = to_core(here, here, 2)
    all_copy.start()
    finished_first(0)
    finished_rest(0)
    finished(send_back, 2, 0)
    wait_bytes(cross_filter, copy_sem.at[4, 0])
    all_copy.wait_recv()
    for copy in (taps_copy, filter_copy, all_copy):
        copy.wait_send()


def finish(
    group,
    queries,
    keys,
    values,
    cotangent,
    back,
    pick,
    gated,
    grad_queries,
    grad_keys,
    grad_values,
    filter_grad,
):
    rows, channels = queries.shape
    lanes = channels // group
    spread = pick[...]
    width = back.shape[2]
    flat = back[...].reshape(2 * group, width)
    for i in range(lanes):
        both = dot(flat[:, i * rows : (i + 1) * rows], spread, (0, 0))
        conv, grad_mixed = both[:, :group], both[:, group:]
        here = pl.ds(i * group, group)
        gated[:, here] = (queries[:, here].astype(F32) * conv).astype(BF16)
        grad_queries[:, here] = (cotangent[:, here].astype(F32) * conv).astype(BF16)
        grad_keys[:, here] = (values[:, here].astype(F32) * grad_mixed).astype(BF16)
        grad_values[:, here] = (keys[:, here].astype(F32) * grad_mixed).astype(BF16)
    flat = flat[:, lanes * rows :]
    first = dot(flat[:, :rows], spread, (0, 0))
    filter_grad[:, pl.ds(0, 2 * group)] = first
    filter_grad[:, pl.ds(2 * group, group)] = dot(flat[:, rows:], spread, (0, 0))[:, :group]


def shards(group, parts, queries, keys, values, filter_taps, cotangent):
    rows, channels = filter_taps.shape
    lanes = channels // group
    tables = constant_tables(group, rows)
    vmem = pltpu.VMEM
    local = (rows, channels)
    block = (group, 2, (lanes + 2) * rows)
    single = (group, 2, 2 * rows)
    half = group // 2
    arrays = (queries[0], keys[0], values[0], filter_taps, cotangent[0])
    back = pl.pallas_call(
        functools.partial(kernel, group, parts),
        out_shape=jax.ShapeDtypeStruct(block, BF16),
        in_specs=[pl.BlockSpec(memory_space=pl.ANY)] * 12,
        out_specs=pl.BlockSpec(memory_space=vmem),
        scratch_shapes=[vmem(local, BF16)] * 5
        + [vmem(table.shape, table.dtype) for table in tables]
        + [vmem(block, BF16)] * 3
        + [vmem(single, BF16)]
        + [vmem((half,) + single[1:], BF16)] * 2
        + [
            vmem((3 * lanes * group, 2 * rows), BF16),
            vmem((3 * lanes * group, 2 * rows), F32),
            vmem((2 * lanes * group, 2 * rows), BF16),
            vmem((4 * group, lanes * rows), BF16),
            pltpu.SemaphoreType.DMA((6,)),
            pltpu.SemaphoreType.DMA((6,)),
            pltpu.SemaphoreType.DMA((5, 2)),
            pltpu.SemaphoreType.DMA((3, 2)),
            pltpu.SemaphoreType.REGULAR,
        ],
        compiler_params=pltpu.CompilerParams(
            collective_id=0, has_side_effects=True, vmem_limit_bytes=60 << 20
        ),
    )(*arrays, *tables)
    outs = pl.pallas_call(
        functools.partial(finish, group),
        out_shape=[jax.ShapeDtypeStruct(local, BF16)] * 4 + [jax.ShapeDtypeStruct(local, F32)],
        in_specs=[pl.BlockSpec(memory_space=vmem)] * 6,
        out_specs=[pl.BlockSpec(memory_space=vmem)] * 5,
        compiler_params=pltpu.CompilerParams(vmem_limit_bytes=60 << 20),
    )(queries[0], keys[0], values[0], cotangent[0], back, tables[4])
    return tuple(out[None] for out in outs[:4]) + (outs[4],)


def solution(mesh):
    spec = P("dp", "ctx", None)
    return jax.shard_map(
        functools.partial(shards, mesh.shape["ctx"], mesh.shape["dp"]),
        mesh=mesh,
        in_specs=(spec, spec, spec, P("ctx", None), spec),
        out_specs=(spec, spec, spec, spec, P("ctx", None)),
        check_vma=False,
    )
```

time: 48.6 us -> 44 us (0.905)
  Pallas kernels: 47.5 us -> 43.2 us
    pallas_call x1, Pallas kernels: 45.1 us -> 40.9 us  [shards(): pl.pallas_call(functools.partial(kernel, group, parts), out_shape=jax.Sha...]
where the time goes in v2:
time: 44 us; the launch traced here: 43.8 us
  Pallas kernels  43.2 us (98%)
  between operations  0.64 us (1%)
    pallas_call x1, Pallas kernels, shards(): pl.pallas_call(functools.partial(kernel, group, parts), out_shape=jax.Sha...  40.9 us
    pallas_call x1, Pallas kernels, shards(): pl.pallas_call(functools.partial(finish, group), out_shape=[jax.ShapeDtyp...  2.3 us

profile of v2, /device:TPU:1, one launch (start us, length us, event | category | flops | bytes accessed | tf_op | source)
XLA Modules:
  0.0 43.8 jit_solution(15267918142121931017)
XLA Ops:
  0.6 40.9 %shard_map.155.back = bf16[128,2,640]{2,1,0:T(2,128)(2,1)} custom-call(bf16[128,384]{1,0:T(8,128)(2,1)} %bitcast.8, bf16[128,384]{1,0:T(8,128)(2,1)} %bitcast.10, bf16[128,384]{1,0:T(8,128)(2,1)} %bitcast.12, bf16[128,384]{1,0:T(8,128)(2,1)} %taps.1, bf16[128,384]{1,0:T(8,128)(2,1)} %bitcast.14, bf16[512,256]{1,0:T(8,128)(2,1)} %constant.14.clone.forward_hbm, ...), custom_call_target="tpu_custom_call" | custom-call | tf_op jit(solution)/shard_map/pallas_call | solution.py:439
  41.5 2.3 %shard_map.156 = (bf16[128,384]{1,0:T(8,128)(2,1)}, bf16[128,384]{1,0:T(8,128)(2,1)}, bf16[128,384]{1,0:T(8,128)(2,1)}, bf16[128,384]{1,0:T(8,128)(2,1)}, f32[128,384]{1,0:T(8,128)}) custom-call(bf16[128,384]{1,0:T(8,128)(2,1)} %bitcast.9, bf16[128,384]{1,0:T(8,128)(2,1)} %bitcast.11, bf16[128,384]{1,0:T(8,128)(2,1)} %bitcast.13, bf16[128,384]{1,0:T(8,128)(2,1)} %bitcast.15, ...), custom_call_target="tpu_custom_call" | custom-call | tf_op jit(solution)/shard_map/pallas_call | solution.py:464

commit v3 on v2

--- a/solution.py
+++ b/solution.py
@@ -40,16 +40,20 @@
     pick = np.zeros((group, 2, 2, group))
     for slot in range(2):
         pick[outer, slot, slot, outer] = 1.0
-    return (
-        jnp.asarray(forward.reshape(4 * group, 2 * group), BF16),
-        jnp.asarray(inverse.reshape(2 * group, 4 * group), BF16),
-        jnp.asarray(inner_forward, BF16),
-        jnp.asarray(inner_inverse, BF16),
-        jnp.asarray(pick.reshape(2 * group, 2 * group), BF16),
-        jnp.asarray(np.cos(angle_twist), F32),
-        jnp.asarray(np.sin(angle_twist), F32),
-    )
-
+    inverse = inverse.reshape(2 * group, 4 * group)
+    squares = [
+        forward.reshape(4 * group, 2 * group),
+        inner_forward,
+        inner_inverse,
+        inverse[:, : 2 * group],
+        inverse[:, 2 * group :],
+        pick.reshape(2 * group, 2 * group),
+    ]
+    twists = np.stack([np.cos(angle_twist), np.sin(angle_twist)])
+    return jnp.asarray(np.concatenate(squares), BF16), jnp.asarray(twists, F32)
+
+
+KERNEL_VMEM = 54613 << 10
 
 GRID = (8, 4, 4)
 
@@ -88,13 +92,15 @@
     values,
     taps,
     cotangent,
-    forward_hbm,
-    inverse_hbm,
-    inner_forward_hbm,
-    inner_inverse_hbm,
-    pick_hbm,
-    twist_cos_hbm,
-    twist_sin_hbm,
+    tables_hbm,
+    twists_hbm,
+    gated,
+    grad_queries,
+    grad_keys,
+    grad_values,
+    filter_first,
+    filter_second,
+    filter_third,
     recv_back,
     q_buf,
     k_buf,
@@ -138,6 +144,17 @@
     lanes = queries.shape[1] // group
     rows = queries.shape[0]
 
+    def table(index):
+        return tables_hbm.at[pl.ds(index * 2 * group, 2 * group)]
+
+    loads = [
+        pltpu.make_async_copy(source, target, in_sem.at[index])
+        for index, (source, target) in enumerate(
+            [(keys, k_buf), (values, v_buf), (queries, q_buf), (cotangent, c_buf), (taps, t_buf), (table(6), pick)]
+        )
+    ]
+    for load in loads:
+        load.start()
     barrier = pltpu.get_barrier_semaphore()
 
     def greet(row, places):
@@ -150,26 +167,22 @@
     others(me, greet, (0, rows_all - 1), True)
     pl.semaphore_signal(barrier, inc=1, device_id=(twin, me), device_id_type=MESH)
 
-    loads = [
-        pltpu.make_async_copy(source, target, in_sem.at[index])
-        for index, (source, target) in enumerate(
-            [(keys, k_buf), (values, v_buf), (queries, q_buf), (cotangent, c_buf), (taps, t_buf), (pick_hbm, pick)]
-        )
-    ]
     tables = [
         pltpu.make_async_copy(source, target, table_sem.at[index])
         for index, (source, target) in enumerate(
             [
-                (forward_hbm, forward),
-                (twist_cos_hbm, twist_cos),
-                (twist_sin_hbm, twist_sin),
-                (inner_forward_hbm, inner_forward),
-                (inner_inverse_hbm, inner_inverse),
-                (inverse_hbm, inverse),
+                (table(0), forward.at[pl.ds(0, 2 * group)]),
+                (table(1), forward.at[pl.ds(2 * group, 2 * group)]),
+                (twists_hbm.at[0], twist_cos),
+                (twists_hbm.at[1], twist_sin),
+                (table(2), inner_forward),
+                (table(3), inner_inverse),
+                (table(4), inverse.at[0]),
+                (table(5), inverse.at[1]),
             ]
         )
     ]
-    for load in loads + tables:
+    for load in tables:
         load.start()
 
     for load in loads:
@@ -293,8 +306,8 @@
     def second(buffer, which):
         return buffer.at[pl.ds(which * half, half), :, pl.ds(width, 2 * rows)]
 
-    for table in tables:
-        table.wait()
+    for load in tables:
+        load.wait()
 
     def twist(real_part, imag_part, slot):
         rows_here = pl.ds(slot * group, group)
@@ -335,7 +348,10 @@
             untwisted[pl.ds(2 * r * group, group), across] = (real_part * cosines - imag_part * sines).astype(BF16)
             untwisted[pl.ds((2 * r + 1) * group, group), across] = (real_part * sines + imag_part * cosines).astype(BF16)
         size = (slots[-1][1] + 1) * rows
-        back = dot(inverse[...], untwisted[:, pl.ds(0, size)]).astype(BF16)
+        back = (
+            dot(inverse[0], untwisted[pl.ds(0, 2 * group), pl.ds(0, size)])
+            + dot(inverse[1], untwisted[pl.ds(2 * group, 2 * group), pl.ds(0, size)])
+        ).astype(BF16)
         target[:, :, pl.ds(0, size)] = back.reshape(group, 2, size)
 
     pair_slots = [(r, j) for r in range(2) for j in range(lanes)]
@@ -384,46 +400,42 @@
     here[...] = (here[...].astype(F32) + cross_filter[...].astype(F32)).astype(BF16)
     all_copy = to_core(here, here, 2)
     all_copy.start()
+    flat = recv_back[:, :, first].reshape(2 * group, width)
+    for i in range(lanes):
+        both = dot(flat[:, i * rows : (i + 1) * rows], spread, (0, 0))
+        conv, grad_mixed = both[:, :group], both[:, group:]
+        here = pl.ds(i * group, group)
+        gated[:, here] = (q_buf[:, here].astype(F32) * conv).astype(BF16)
+        grad_queries[:, here] = (c_buf[:, here].astype(F32) * conv).astype(BF16)
+        grad_keys[:, here] = (v_buf[:, here].astype(F32) * grad_mixed).astype(BF16)
+        grad_values[:, here] = (k_buf[:, here].astype(F32) * grad_mixed).astype(BF16)
+    all_copy.wait_recv()
+    flat = recv_back[:, :, rest].reshape(2 * group, 2 * rows)
+    both = dot(flat[:, :rows], spread, (0, 0))
+    filter_first[...] = both[:, :group]
+    filter_second[...] = both[:, group:]
+    filter_third[...] = dot(flat[:, rows:], spread, (0, 0))[:, :group]
     finished_first(0)
     finished_rest(0)
     finished(send_back, 2, 0)
     wait_bytes(cross_filter, copy_sem.at[4, 0])
-    all_copy.wait_recv()
     for copy in (taps_copy, filter_copy, all_copy):
         copy.wait_send()
 
 
-def finish(
-    group,
-    queries,
-    keys,
-    values,
-    cotangent,
-    back,
-    pick,
-    gated,
-    grad_queries,
-    grad_keys,
-    grad_values,
-    filter_grad,
-):
-    rows, channels = queries.shape
-    lanes = channels // group
-    spread = pick[...]
-    width = back.shape[2]
-    flat = back[...].reshape(2 * group, width)
-    for i in range(lanes):
-        both = dot(flat[:, i * rows : (i + 1) * rows], spread, (0, 0))
-        conv, grad_mixed = both[:, :group], both[:, group:]
-        here = pl.ds(i * group, group)
-        gated[:, here] = (queries[:, here].astype(F32) * conv).astype(BF16)
-        grad_queries[:, here] = (cotangent[:, here].astype(F32) * conv).astype(BF16)
-        grad_keys[:, here] = (values[:, here].astype(F32) * grad_mixed).astype(BF16)
-        grad_values[:, here] = (keys[:, here].astype(F32) * grad_mixed).astype(BF16)
-    flat = flat[:, lanes * rows :]
-    first = dot(flat[:, :rows], spread, (0, 0))
-    filter_grad[:, pl.ds(0, 2 * group)] = first
-    filter_grad[:, pl.ds(2 * group, group)] = dot(flat[:, rows:], spread, (0, 0))[:, :group]
+def hand_over(gated, grad_queries, grad_keys, grad_values, first, second, third, *refs):
+    *targets, filter_grad, sems = refs
+    group = first.shape[1]
+    pairs = list(zip((gated, grad_queries, grad_keys, grad_values), targets))
+    for index, source in enumerate((first, second, third)):
+        pairs.append((source, filter_grad.at[:, pl.ds(index * group, group)]))
+    copies = [
+        pltpu.make_async_copy(source, target, sems.at[index]) for index, (source, target) in enumerate(pairs)
+    ]
+    for copy in copies:
+        copy.start()
+    for copy in copies:
+        copy.wait()
 
 
 def shards(group, parts, queries, keys, values, filter_taps, cotangent):
@@ -436,13 +448,17 @@
     single = (group, 2, 2 * rows)
     half = group // 2
     arrays = (queries[0], keys[0], values[0], filter_taps, cotangent[0])
-    back = pl.pallas_call(
+    results = [jax.ShapeDtypeStruct(local, BF16)] * 4 + [jax.ShapeDtypeStruct(local, F32)]
+    outs = pl.pallas_call(
         functools.partial(kernel, group, parts),
-        out_shape=jax.ShapeDtypeStruct(block, BF16),
-        in_specs=[pl.BlockSpec(memory_space=pl.ANY)] * 12,
-        out_specs=pl.BlockSpec(memory_space=vmem),
-        scratch_shapes=[vmem(local, BF16)] * 5
-        + [vmem(table.shape, table.dtype) for table in tables]
+        out_shape=results[:4] + [jax.ShapeDtypeStruct((rows, group), F32)] * lanes,
+        in_specs=[pl.BlockSpec(memory_space=pl.ANY)] * 7,
+        out_specs=[pl.BlockSpec(memory_space=vmem)] * (4 + lanes),
+        scratch_shapes=[vmem(block, BF16)]
+        + [vmem(local, BF16)] * 5
+        + [vmem((4 * group, 2 * group), BF16), vmem((2, 2 * group, 2 * group), BF16)]
+        + [vmem((2 * group, 2 * group), BF16)] * 3
+        + [vmem((group, rows), F32)] * 2
         + [vmem(block, BF16)] * 3
         + [vmem(single, BF16)]
         + [vmem((half,) + single[1:], BF16)] * 2
@@ -452,22 +468,23 @@
             vmem((2 * lanes * group, 2 * rows), BF16),
             vmem((4 * group, lanes * rows), BF16),
             pltpu.SemaphoreType.DMA((6,)),
-            pltpu.SemaphoreType.DMA((6,)),
+            pltpu.SemaphoreType.DMA((8,)),
             pltpu.SemaphoreType.DMA((5, 2)),
             pltpu.SemaphoreType.DMA((3, 2)),
             pltpu.SemaphoreType.REGULAR,
         ],
         compiler_params=pltpu.CompilerParams(
-            collective_id=0, has_side_effects=True, vmem_limit_bytes=60 << 20
+            collective_id=0, has_side_effects=True, vmem_limit_bytes=KERNEL_VMEM
         ),
     )(*arrays, *tables)
     outs = pl.pallas_call(
-        functools.partial(finish, group),
-        out_shape=[jax.ShapeDtypeStruct(local, BF16)] * 4 + [jax.ShapeDtypeStruct(local, F32)],
-        in_specs=[pl.BlockSpec(memory_space=vmem)] * 6,
-        out_specs=[pl.BlockSpec(memory_space=vmem)] * 5,
-        compiler_params=pltpu.CompilerParams(vmem_limit_bytes=60 << 20),
-    )(queries[0], keys[0], values[0], cotangent[0], back, tables[4])
+        hand_over,
+        out_shape=results,
+        in_specs=[pl.BlockSpec(memory_space=vmem)] * (4 + lanes),
+        out_specs=[pl.BlockSpec(memory_space=pl.ANY)] * 5,
+        scratch_shapes=[pltpu.SemaphoreType.DMA((4 + lanes,))],
+        compiler_params=pltpu.CompilerParams(vmem_limit_bytes=16 << 20),
+    )(*outs)
     return tuple(out[None] for out in outs[:4]) + (outs[4],)
 
 

time: 44 us -> 42.1 us (0.957)
  Pallas kernels: 43.2 us -> 41.3 us
    pallas_call x2, Pallas kernels: 43.2 us -> 41.3 us  [the longest x1 40.5 us: shards(): pl.pallas_call(functools.partial(kernel, group, parts), out_shape=results...]
where the time goes in v3:
time: 42.1 us; the launch traced here: 42 us
  Pallas kernels  41.3 us (98%)
  between operations  0.64 us (2%)
    pallas_call x1, Pallas kernels, shards(): pl.pallas_call(functools.partial(kernel, group, parts), out_shape=results...  40.5 us
    pallas_call x1, Pallas kernels, shards(): pl.pallas_call(hand_over, out_shape=results, in_specs=[pl.BlockSpec(memor...  0.87 us

profile of v3, /device:TPU:1, one launch (start us, length us, event | category | flops | bytes accessed | tf_op | source)
XLA Modules:
  0.0 42.0 jit_solution(13935157812492268489)
XLA Ops:
  0.6 40.5 %shard_map.110 = (bf16[128,384]{1,0:T(8,128)(2,1)S(1)}, bf16[128,384]{1,0:T(8,128)(2,1)S(1)}, bf16[128,384]{1,0:T(8,128)(2,1)S(1)}, bf16[128,384]{1,0:T(8,128)(2...) custom-call(bf16[128,384]{1,0:T(8,128)(2,1)} %bitcast.8, ...), custom_call_target="tpu_custom_call" | custom-call | tf_op jit(solution)/shard_map/pallas_call | solution.py:452
  41.1 0.9 %shard_map.111 = (bf16[128,384]{1,0:T(8,128)(2,1)}, bf16[128,384]{1,0:T(8,128)(2,1)}, bf16[128,384]{1,0:T(8,128)(2,1)}, bf16[128,384]{1,0:T(8,128)(2,1)}, f32[128,384]{1,0:T(8,128)}) custom-call(bf16[128,384]{1,0:T(8,128)(2,1)S(1)} %get-tuple-element.17.gated, bf16[128,384]{1,0:T(8,128)(2,1)S(1)} %get-tuple-element.18.grad_queries, ...), custom_call_target="tpu_custom_call" | custom-call | tf_op jit(solution)/shard_map/pallas_call | solution.py:480

commit v4 on v3

--- a/solution.py
+++ b/solution.py
@@ -257,12 +257,18 @@
     def wait_bytes(some, sem):
         pltpu.make_async_copy(some, some, sem).wait()
 
-    def finished(buffer, index, side):
+    def finished_whole(buffer, index, side):
         for value in range(2):
 
             @pl.when(core == value)
             def _():
                 wait_bytes(buffer.at[pl.ds(0, half - 1 + value)], copy_sem.at[index, side])
+
+    def finished_parts(buffer, index, side):
+        for value in range(2):
+
+            @pl.when(core == value)
+            def _():
                 wait_bytes(buffer.at[pl.ds(0, half - value), :, pl.ds(0, width)], copy_sem.at[index + 1, side])
 
     first, rest = pl.ds(0, width), pl.ds(width, 2 * rows)
@@ -374,16 +380,13 @@
     send_back[pl.ds(mine * half, half), :, rest] = both.astype(BF16)
     pl.semaphore_wait(ready_sem, 1)
 
-    def cross(row, places):
-        @pl.when(row // (rows_all // 2) == mine)
-        def _():
-            for place in places:
-                peer = row * plane + place
-                remote(
-                    send_back.at[peer, :, rest], cross_filter.at[lax.rem(me, half)], mate, peer, 4
-                ).start()
-
-    others(me, cross, (0, rows_all), False)
+    lines = rows_all // 2
+    line = lax.rem(me // plane, lines)
+    for step in range(lines):
+        row = mine * lines + lax.rem(line + step, lines)
+        for place in planes(me):
+            peer = row * plane + place
+            remote(send_back.at[peer, :, rest], cross_filter.at[lax.rem(me, half)], mate, peer, 4).start()
 
     taps_copy.wait_recv()
     stage_forward(recv_there[:, :, rest], tap_slots, 2 * lanes)
@@ -394,12 +397,13 @@
     keep_own(send_back, recv_back)
     exchange(send_back, recv_back, 2, (0, rows_all - 1), True)
 
-    finished(recv_back, 2, 1)
+    finished_whole(recv_back, 2, 1)
     wait_bytes(cross_filter, copy_sem.at[4, 1])
     here = second(recv_back, mine)
     here[...] = (here[...].astype(F32) + cross_filter[...].astype(F32)).astype(BF16)
     all_copy = to_core(here, here, 2)
     all_copy.start()
+    finished_parts(recv_back, 2, 1)
     flat = recv_back[:, :, first].reshape(2 * group, width)
     for i in range(lanes):
         both = dot(flat[:, i * rows : (i + 1) * rows], spread, (0, 0))
@@ -417,7 +421,8 @@
     filter_third[...] = dot(flat[:, rows:], spread, (0, 0))[:, :group]
     finished_first(0)
     finished_rest(0)
-    finished(send_back, 2, 0)
+    finished_whole(send_back, 2, 0)
+    finished_parts(send_back, 2, 0)
     wait_bytes(cross_filter, copy_sem.at[4, 0])
     for copy in (taps_copy, filter_copy, all_copy):
         copy.wait_send()

time: 42.1 us -> 41.4 us (0.983)
  Pallas kernels: 41.3 us -> 40.6 us
    pallas_call x1, Pallas kernels: 40.5 us -> 39.8 us  [shards(): pl.pallas_call(functools.partial(kernel, group, parts), out_shape=results...]
where the time goes in v4:
time: 41.4 us; the launch traced here: 41.3 us
  Pallas kernels  40.6 us (98%)
  between operations  0.64 us (2%)
    pallas_call x1, Pallas kernels, shards(): pl.pallas_call(functools.partial(kernel, group, parts), out_shape=results...  39.8 us
    pallas_call x1, Pallas kernels, shards(): pl.pallas_call(hand_over, out_shape=results, in_specs=[pl.BlockSpec(memor...  0.87 us

profile of v4, /device:TPU:1, one launch (start us, length us, event | category | flops | bytes accessed | tf_op | source)
XLA Modules:
  0.0 41.3 jit_solution(4455865875356006632)
XLA Ops:
  0.6 39.8 %shard_map.110 = (bf16[128,384]{1,0:T(8,128)(2,1)S(1)}, bf16[128,384]{1,0:T(8,128)(2,1)S(1)}, bf16[128,384]{1,0:T(8,128)(2,1)S(1)}, bf16[128,384]{1,0:T(8,128)(2...) custom-call(bf16[128,384]{1,0:T(8,128)(2,1)} %bitcast.8, ...), custom_call_target="tpu_custom_call" | custom-call | tf_op jit(solution)/shard_map/pallas_call | solution.py:457
  40.4 0.9 %shard_map.111 = (bf16[128,384]{1,0:T(8,128)(2,1)}, bf16[128,384]{1,0:T(8,128)(2,1)}, bf16[128,384]{1,0:T(8,128)(2,1)}, bf16[128,384]{1,0:T(8,128)(2,1)}, f32[128,384]{1,0:T(8,128)}) custom-call(bf16[128,384]{1,0:T(8,128)(2,1)S(1)} %get-tuple-element.17.gated, bf16[128,384]{1,0:T(8,128)(2,1)S(1)} %get-tuple-element.18.grad_queries, ...), custom_call_target="tpu_custom_call" | custom-call | tf_op jit(solution)/shard_map/pallas_call | solution.py:485

commit v5 on v4

--- a/solution.py
+++ b/solution.py
@@ -236,23 +236,23 @@
         )
 
     def exchange(source, target, index, steps, own_row):
-        def send(row, places):
-            whole = row // (rows_all // 2) == mine
-
-            @pl.when(whole)
+        def send_whole(row, places):
+            @pl.when(row // (rows_all // 2) == mine)
             def _():
                 for place in places:
                     peer = row * plane + place
                     remote(source.at[peer], target.at[me], part, peer, index).start()
 
-            @pl.when(jnp.logical_not(whole))
+        def send_part(row, places):
+            @pl.when(row // (rows_all // 2) != mine)
             def _():
                 here = pl.ds(0, width)
                 for place in places:
                     peer = row * plane + place
                     remote(source.at[peer, :, here], target.at[me, :, here], part, peer, index + 1).start()
 
-        others(me, send, steps, own_row)
+        others(me, send_whole, steps, own_row)
+        others(me, send_part, steps, own_row)
 
     def wait_bytes(some, sem):
         pltpu.make_async_copy(some, some, sem).wait()

time: 41.4 us -> 41.4 us (level)
  no operation moved by 1% of the time
where the time goes in v5:
time: 41.4 us; the launch traced here: 41.3 us
  Pallas kernels  40.6 us (98%)
  between operations  0.64 us (2%)
    pallas_call x1, Pallas kernels, shards(): pl.pallas_call(functools.partial(kernel, group, parts), out_shape=results...  39.8 us
    pallas_call x1, Pallas kernels, shards(): pl.pallas_call(hand_over, out_shape=results, in_specs=[pl.BlockSpec(memor...  0.87 us

profile of v5, /device:TPU:1, one launch (start us, length us, event | category | flops | bytes accessed | tf_op | source)
XLA Modules:
  0.0 41.3 jit_solution(4735660903352445590)
XLA Ops:
  0.6 39.8 %shard_map.110 = (bf16[128,384]{1,0:T(8,128)(2,1)S(1)}, bf16[128,384]{1,0:T(8,128)(2,1)S(1)}, bf16[128,384]{1,0:T(8,128)(2,1)S(1)}, bf16[128,384]{1,0:T(8,128)(2...) custom-call(bf16[128,384]{1,0:T(8,128)(2,1)} %bitcast.8, ...), custom_call_target="tpu_custom_call" | custom-call | tf_op jit(solution)/shard_map/pallas_call | solution.py:457
  40.4 0.9 %shard_map.111 = (bf16[128,384]{1,0:T(8,128)(2,1)}, bf16[128,384]{1,0:T(8,128)(2,1)}, bf16[128,384]{1,0:T(8,128)(2,1)}, bf16[128,384]{1,0:T(8,128)(2,1)}, f32[128,384]{1,0:T(8,128)}) custom-call(bf16[128,384]{1,0:T(8,128)(2,1)S(1)} %get-tuple-element.17.gated, bf16[128,384]{1,0:T(8,128)(2,1)S(1)} %get-tuple-element.18.grad_queries, ...), custom_call_target="tpu_custom_call" | custom-call | tf_op jit(solution)/shard_map/pallas_call | solution.py:485
